TPU v7x, 32 devices: a whole 2x2x4 slice. The times are simulated.
32 devices in a mesh: grp: 4 (over x, core), sub: 8 (over z, y).
Axes of the slice: x: 2, y: 2, z: 4, core: 2. Of those that a mesh axis runs over, the one named last changes fastest.
Arguments:
- right_side: float32 [65536, 128], P(('grp', 'sub')), may hold values from -6 to 6
- fine_values: float32 [81, 65536], P(None, ('grp', 'sub')), as said below
- columns: int32 [81, 65536], P(None, ('grp', 'sub')), may hold values from 0 to 2175, as said below
- agg_map: int32 [65536], P(('grp', 'sub')), may hold values from 0 to 127
- send_lo: int32 [2048], P(('grp', 'sub')), may hold values from 0 to 2047
- send_hi: int32 [2048], P(('grp', 'sub')), may hold values from 0 to 2047
- coarse_matrix: float32 [4, 1024, 1024], P('grp', 'sub'), as said below
Outputs:
- solution: float32 [65536, 128], P(('grp', 'sub'))
- residual: float32 [65536, 128], P(('grp', 'sub'))
Inputs may be any that keep to these rules, and one draw needn't show every extreme that they name: `columns`: entry 0 of row i of a partition is 64 + i, the others lie within 64 positions of it. `fine_values`: entry 0 lies in 2.5 to 5 and every other entry's magnitude is at most 0.06. `coarse_matrix`: symmetric; the diagonal lies in 10 to 20, other entries' magnitudes are at most 7.1 / sqrt(1024).
All inputs are finite; a program needn't handle non-finite values.
Results may differ from a plain program's by a relative error of at most 0.0001.
Values sent between devices are 32-bit elements; how exact they have to be, the bound alone decides.
A program may use at most 128 MiB of HBM per device.

v0:
```python
import jax
import jax.numpy as jnp
from jax import lax
from jax.sharding import PartitionSpec as P

CHEB_FINE = 2
CHEB_COARSE = 6
CYCLES = 2


THETA = 1.0
DELTA = 0.7
OMEGA = 0.6
highest = lax.Precision.HIGHEST


def from_behind(shard, axis, by):
    peers = lax.axis_size(axis)
    pairs = [(i, i + by) for i in range(peers) if 0 <= i + by < peers]
    return lax.ppermute(shard, axis, pairs)


def band_tiles(fine_values, columns, block_rows):
    rows_dev = columns.shape[1]
    rows = jnp.arange(rows_dev, dtype=jnp.int32)
    starts = rows // block_rows * block_rows
    local = columns - starts[None, :]
    places = jnp.arange(2 * block_rows, dtype=jnp.int32)[None, :]
    tiles = jnp.zeros((rows_dev, 2 * block_rows), jnp.float32)
    for entry in range(columns.shape[0]):
        tiles = tiles + jnp.where(local[entry][:, None] == places, fine_values[entry][:, None], 0.0)
    tiles = tiles.reshape(rows_dev // block_rows, block_rows, 2 * block_rows)
    return (tiles[:, :, :block_rows], tiles[:, :, block_rows:])


def selector(indices, count):
    return (indices[:, None] == jnp.arange(count, dtype=jnp.int32)[None, :]).astype(jnp.float32)


def fine_apply(vector, low_tiles, high_tiles, pick_lo, pick_hi):
    upper_rows = jnp.dot(pick_hi, vector, precision=highest)
    lower_rows = jnp.dot(pick_lo, vector, precision=highest)
    below = from_behind(upper_rows, ("grp", "sub"), 1)
    above = from_behind(lower_rows, ("grp", "sub"), -1)
    extended = jnp.concatenate([below, vector, above], 0)
    block_rows = low_tiles.shape[1]
    pieces = extended.reshape(-1, block_rows, vector.shape[1])
    total = jnp.einsum("brc,bcn->brn", low_tiles, pieces[:-1], precision=highest)
    total = total + jnp.einsum("brc,bcn->brn", high_tiles, pieces[1:], precision=highest)
    return total.reshape(vector.shape)


def chebyshev(residual, apply, inverse, steps, final):
    rho_old = DELTA / THETA
    direction = inverse * residual / THETA
    result = direction
    for turn in range(1, steps):
        residual = residual - apply(direction)
        rho_new = 1.0 / (2.0 * THETA / DELTA - rho_old)
        direction = rho_new * rho_old * direction + 2.0 * rho_new / DELTA * inverse * residual
        result = result + direction
        rho_old = rho_new
    if final:
        residual = residual - apply(direction)
    return (result, residual)


def body(right_side, fine_values, columns, agg_map, send_lo, send_hi, coarse_matrix):
    rows_dev = right_side.shape[0]
    low_tiles, high_tiles = band_tiles(fine_values, columns, 2 * send_lo.shape[0])
    pick_lo = selector(send_lo, rows_dev)
    pick_hi = selector(send_hi, rows_dev)

    def apply_fine(vector):
        return fine_apply(vector, low_tiles, high_tiles, pick_lo, pick_hi)

    own_rows = coarse_matrix[0]
    aggregates = own_rows.shape[0]
    sub_index = lax.axis_index("sub")
    start = sub_index * aggregates
    block = lax.dynamic_slice_in_dim(own_rows, start, aggregates, 1)
    coarse_inverse = 1.0 / jnp.diagonal(block)[:, None]

    def apply_coarse(vector):
        whole = lax.all_gather(vector, "sub", axis=0, tiled=True)
        return jnp.dot(own_rows, whole, precision=highest)

    dinv = 1.0 / fine_values[0][:, None]
    onehot = selector(agg_map, aggregates)
    solution = jnp.zeros_like(right_side)
    residual = right_side
    for cycle in range(CYCLES):
        update, residual = chebyshev(residual, apply_fine, dinv, CHEB_FINE, True)
        solution = solution + update
        smoothed = residual - OMEGA * apply_fine(dinv * residual)
        coarse_rhs = jnp.einsum("ra,rn->an", onehot, smoothed, precision=highest)
        result, unused = chebyshev(coarse_rhs, apply_coarse, coarse_inverse, CHEB_COARSE, False)
        spread = jnp.dot(onehot, result, precision=highest)
        correction = spread - OMEGA * dinv * apply_fine(spread)
        solution = solution + correction
        residual = residual - apply_fine(correction)
        update, residual = chebyshev(residual, apply_fine, dinv, CHEB_FINE, True)
        solution = solution + update
    return (solution, residual)


def solution(mesh):
    placed = (
        P(("grp", "sub"), None),
        P(None, ("grp", "sub")),
        P(None, ("grp", "sub")),
        P(("grp", "sub")),
        P(("grp", "sub")),
        P(("grp", "sub")),
        P("grp", "sub", None),
    )
    return jax.shard_map(
        body,
        mesh=mesh,
        in_specs=placed,
        out_specs=(P(("grp", "sub"), None), P(("grp", "sub"), None)),
        check_vma=False,
    )
```

profile of v0, /device:TPU:2, one launch (start us, length us, event | category | flops | bytes accessed | tf_op | source)
XLA Modules:
  0.0 594.3 jit_solution(620123093191027239)
XLA Ops:
  0.7 1.7 fusion.141
  2.4 2.5 fusion.51
  4.9 5.9 collective-permute-start.1
  10.8 2.5 fusion.65
  13.3 2.0 collective-permute-start
  20.3 47.5 %select_add_fusion = f32[16,128,256]{2,1,0:T(8,128)S(1)} fusion(f32[16,128]{1,0:T(8,128)S(1)} %bitcast.486, s32[16,128]{1,0:T(8,128)} %bitcast.608, f32[16,128]{1,0:T(8,128)S(1)} %bitcast.487, s32[16,128]{1,0:T(8,128)} %bitcast.609, f32[16,128]{1,0:T(8,128)S(1)} %bitcast.465, s32[16,128]{1,0:T(8,128)} %bitcast.610, f32[16,128]{1,0:T(8,128)S(1)} %bitcast.466, ...), kind=kLoop, calls=%fused_computation.1 | loop fusion | flops 126877696 | bytes 3424256 | tf_op jit(solution)/shard_map/add | solution.py:31
  69.1 1.7 pad_maximum_fusion.27
  75.2 2.4 collective-permute-start.2
  77.5 6.8 %collective-permute-start.3 = (f32[64,128]{1,0:T(8,128)S(1)}, f32[64,128]{1,0:T(8,128)S(1)}, u32[]{:S(2)}, u32[]{:S(2)}) collective-permute-start(f32[64,128]{1,0:T(8,128)S(1)} %fusion.50), channel_id=1, source_target_pairs={{1,0},{2,1},{3,2},{4,3},{5,4},{6,5},{7,6},{8,7},{9,8},{10,9},{11,1... | collective-permute-start | bytes 98312 | tf_op jit(solution)/shard_map/ppermute | solution.py:20
  90.1 1.9 collective-permute-start.4
  92.0 7.7 %collective-permute-start.5 = (f32[64,128]{1,0:T(8,128)S(1)}, f32[64,128]{1,0:T(8,128)S(1)}, u32[]{:S(2)}, u32[]{:S(2)}) collective-permute-start(f32[64,128]{1,0:T(8,128)S(1)} %fusion.49), channel_id=1, source_target_pairs={{1,0},{2,1},{3,2},{4,3},{5,4},{6,5},{7,6},{8,7},{9,8},{10,9},{11,1... | collective-permute-start | bytes 98312 | tf_op jit(solution)/shard_map/ppermute | solution.py:20
  105.5 31.6 %all_gather.30 = f32[1024,128]{1,0:T(8,128)S(1)} all-gather(f32[128,128]{1,0:T(8,128)S(1)} %get-tuple-element.209), channel_id=1, replica_groups=mesh['grp'=4,'sub'=8] {'sub'}, dimensions={0}, use_global_device_ids=true | all-gather | bytes 589824 | tf_op jit(solution)/shard_map/all_gather | solution.py:85
  137.7 31.3 %all_gather.31 = f32[1024,128]{1,0:T(8,128)S(1)} all-gather(f32[128,128]{1,0:T(8,128)S(1)} %get-tuple-element.211), channel_id=1, replica_groups=mesh['grp'=4,'sub'=8] {'sub'}, dimensions={0}, use_global_device_ids=true | all-gather | bytes 589824 | tf_op jit(solution)/shard_map/all_gather | solution.py:85
  169.7 31.3 %all_gather.32 = f32[1024,128]{1,0:T(8,128)S(1)} all-gather(f32[128,128]{1,0:T(8,128)S(1)} %get-tuple-element.213), channel_id=1, replica_groups=mesh['grp'=4,'sub'=8] {'sub'}, dimensions={0}, use_global_device_ids=true | all-gather | bytes 589824 | tf_op jit(solution)/shard_map/all_gather | solution.py:85
  201.6 31.4 %all_gather.33 = f32[1024,128]{1,0:T(8,128)S(1)} all-gather(f32[128,128]{1,0:T(8,128)S(1)} %get-tuple-element.215), channel_id=1, replica_groups=mesh['grp'=4,'sub'=8] {'sub'}, dimensions={0}, use_global_device_ids=true | all-gather | bytes 589824 | tf_op jit(solution)/shard_map/all_gather | solution.py:85
  233.6 31.2 %all_gather.34 = f32[1024,128]{1,0:T(8,128)S(1)} all-gather(f32[128,128]{1,0:T(8,128)S(1)} %get-tuple-element.217), channel_id=1, replica_groups=mesh['grp'=4,'sub'=8] {'sub'}, dimensions={0}, use_global_device_ids=true | all-gather | bytes 589824 | tf_op jit(solution)/shard_map/all_gather | solution.py:85
  267.5 3.6 collective-permute-start.6
  271.1 5.8 collective-permute-start.7
  282.4 1.9 collective-permute-start.8
  284.3 7.2 %collective-permute-start.9 = (f32[64,128]{1,0:T(8,128)S(1)}, f32[64,128]{1,0:T(8,128)S(1)}, u32[]{:S(2)}, u32[]{:S(2)}) collective-permute-start(f32[64,128]{1,0:T(8,128)S(1)} %fusion.47), channel_id=1, source_target_pairs={{1,0},{2,1},{3,2},{4,3},{5,4},{6,5},{7,6},{8,7},{9,8},{10,9},{11,1... | collective-permute-start | bytes 98312 | tf_op jit(solution)/shard_map/ppermute | solution.py:20
  291.6 1.6 collective-permute-done.9
  297.2 1.9 collective-permute-start.10
  299.1 7.5 %collective-permute-start.11 = (f32[64,128]{1,0:T(8,128)S(1)}, f32[64,128]{1,0:T(8,128)S(1)}, u32[]{:S(2)}, u32[]{:S(2)}) collective-permute-start(f32[64,128]{1,0:T(8,128)S(1)} %fusion.46), channel_id=1, source_target_pairs={{1,0},{2,1},{3,2},{4,3},{5,4},{6,5},{7,6},{8,7},{9,8},{10,9},{11,1... | collective-permute-start | bytes 98312 | tf_op jit(solution)/shard_map/ppermute | solution.py:20
  312.0 1.9 collective-permute-start.12
  313.9 7.2 %collective-permute-start.13 = (f32[64,128]{1,0:T(8,128)S(1)}, f32[64,128]{1,0:T(8,128)S(1)}, u32[]{:S(2)}, u32[]{:S(2)}) collective-permute-start(f32[64,128]{1,0:T(8,128)S(1)} %fusion.45), channel_id=1, source_target_pairs={{1,0},{2,1},{3,2},{4,3},{5,4},{6,5},{7,6},{8,7},{9,8},{10,9},{11,1... | collective-permute-start | bytes 98312 | tf_op jit(solution)/shard_map/ppermute | solution.py:20
  321.2 1.6 collective-permute-done.13
  326.8 1.9 collective-permute-start.14
  328.7 7.5 %collective-permute-start.15 = (f32[64,128]{1,0:T(8,128)S(1)}, f32[64,128]{1,0:T(8,128)S(1)}, u32[]{:S(2)}, u32[]{:S(2)}) collective-permute-start(f32[64,128]{1,0:T(8,128)S(1)} %fusion.44), channel_id=1, source_target_pairs={{1,0},{2,1},{3,2},{4,3},{5,4},{6,5},{7,6},{8,7},{9,8},{10,9},{11,1... | collective-permute-start | bytes 98312 | tf_op jit(solution)/shard_map/ppermute | solution.py:20
  341.7 1.9 collective-permute-start.16
  343.6 7.2 %collective-permute-start.17 = (f32[64,128]{1,0:T(8,128)S(1)}, f32[64,128]{1,0:T(8,128)S(1)}, u32[]{:S(2)}, u32[]{:S(2)}) collective-permute-start(f32[64,128]{1,0:T(8,128)S(1)} %fusion.43), channel_id=1, source_target_pairs={{1,0},{2,1},{3,2},{4,3},{5,4},{6,5},{7,6},{8,7},{9,8},{10,9},{11,1... | collective-permute-start | bytes 98312 | tf_op jit(solution)/shard_map/ppermute | solution.py:20
  350.8 1.6 collective-permute-done.17
  356.5 1.9 collective-permute-start.18
  358.4 7.7 %collective-permute-start.19 = (f32[64,128]{1,0:T(8,128)S(1)}, f32[64,128]{1,0:T(8,128)S(1)}, u32[]{:S(2)}, u32[]{:S(2)}) collective-permute-start(f32[64,128]{1,0:T(8,128)S(1)} %fusion.42), channel_id=1, source_target_pairs={{1,0},{2,1},{3,2},{4,3},{5,4},{6,5},{7,6},{8,7},{9,8},{10,9},{11,1... | collective-permute-start | bytes 98312 | tf_op jit(solution)/shard_map/ppermute | solution.py:20
  371.4 31.2 %all_gather.35 = f32[1024,128]{1,0:T(8,128)S(1)} all-gather(f32[128,128]{1,0:T(8,128)S(1)} %get-tuple-element.219), channel_id=1, replica_groups=mesh['grp'=4,'sub'=8] {'sub'}, dimensions={0}, use_global_device_ids=true | all-gather | bytes 589824 | tf_op jit(solution)/shard_map/all_gather | solution.py:85
  403.2 31.5 %all_gather.36 = f32[1024,128]{1,0:T(8,128)S(1)} all-gather(f32[128,128]{1,0:T(8,128)S(1)} %get-tuple-element.221), channel_id=1, replica_groups=mesh['grp'=4,'sub'=8] {'sub'}, dimensions={0}, use_global_device_ids=true | all-gather | bytes 589824 | tf_op jit(solution)/shard_map/all_gather | solution.py:85
  435.4 31.5 %all_gather.37 = f32[1024,128]{1,0:T(8,128)S(1)} all-gather(f32[128,128]{1,0:T(8,128)S(1)} %get-tuple-element.223), channel_id=1, replica_groups=mesh['grp'=4,'sub'=8] {'sub'}, dimensions={0}, use_global_device_ids=true | all-gather | bytes 589824 | tf_op jit(solution)/shard_map/all_gather | solution.py:85
  467.5 31.5 %all_gather.38 = f32[1024,128]{1,0:T(8,128)S(1)} all-gather(f32[128,128]{1,0:T(8,128)S(1)} %get-tuple-element.225), channel_id=1, replica_groups=mesh['grp'=4,'sub'=8] {'sub'}, dimensions={0}, use_global_device_ids=true | all-gather | bytes 589824 | tf_op jit(solution)/shard_map/all_gather | solution.py:85
  499.6 31.2 %all_gather.39 = f32[1024,128]{1,0:T(8,128)S(1)} all-gather(f32[128,128]{1,0:T(8,128)S(1)} %get-tuple-element.227), channel_id=1, replica_groups=mesh['grp'=4,'sub'=8] {'sub'}, dimensions={0}, use_global_device_ids=true | all-gather | bytes 589824 | tf_op jit(solution)/shard_map/all_gather | solution.py:85
  533.6 1.9 collective-permute-start.20
  535.5 7.4 %collective-permute-start.21 = (f32[64,128]{1,0:T(8,128)S(1)}, f32[64,128]{1,0:T(8,128)S(1)}, u32[]{:S(2)}, u32[]{:S(2)}) collective-permute-start(f32[64,128]{1,0:T(8,128)S(1)} %fusion.41), channel_id=1, source_target_pairs={{1,0},{2,1},{3,2},{4,3},{5,4},{6,5},{7,6},{8,7},{9,8},{10,9},{11,1... | collective-permute-start | bytes 98312 | tf_op jit(solution)/shard_map/ppermute | solution.py:20
  548.4 1.9 collective-permute-start.22
  550.3 7.2 %collective-permute-start.23 = (f32[64,128]{1,0:T(8,128)S(1)}, f32[64,128]{1,0:T(8,128)S(1)}, u32[]{:S(2)}, u32[]{:S(2)}) collective-permute-start(f32[64,128]{1,0:T(8,128)S(1)} %fusion.40), channel_id=1, source_target_pairs={{1,0},{2,1},{3,2},{4,3},{5,4},{6,5},{7,6},{8,7},{9,8},{10,9},{11,1... | collective-permute-start | bytes 98312 | tf_op jit(solution)/shard_map/ppermute | solution.py:20
  557.6 1.6 collective-permute-done.23
  563.2 1.9 collective-permute-start.24
  565.2 7.6 %collective-permute-start.25 = (f32[64,128]{1,0:T(8,128)S(1)}, f32[64,128]{1,0:T(8,128)S(1)}, u32[]{:S(2)}, u32[]{:S(2)}) collective-permute-start(f32[64,128]{1,0:T(8,128)S(1)} %fusion.39), channel_id=1, source_target_pairs={{1,0},{2,1},{3,2},{4,3},{5,4},{6,5},{7,6},{8,7},{9,8},{10,9},{11,1... | collective-permute-start | bytes 98312 | tf_op jit(solution)/shard_map/ppermute | solution.py:20
  576.7 1.8 add_add_fusion
  579.6 1.9 collective-permute-start.26
  581.6 7.2 %collective-permute-start.27 = (f32[64,128]{1,0:T(8,128)S(1)}, f32[64,128]{1,0:T(8,128)S(1)}, u32[]{:S(2)}, u32[]{:S(2)}) collective-permute-start(f32[64,128]{1,0:T(8,128)S(1)} %fusion.38), channel_id=1, source_target_pairs={{1,0},{2,1},{3,2},{4,3},{5,4},{6,5},{7,6},{8,7},{9,8},{10,9},{11,1... | collective-permute-start | bytes 98312 | tf_op jit(solution)/shard_map/ppermute | solution.py:20
  (152 shorter events, 85.7 us)
Async XLA Ops:
  0.6 19.6 %copy-start = (f32[1,128,1024]{2,1,0:T(8,128)S(1)}, f32[1,128,1024]{2,1,0:T(8,128)}, u32[]{:S(2)}) copy-start(f32[1,128,1024]{2,1,0:T(8,128)} %param.13) | copy-start | bytes 1572868
  0.6 14.7 %copy-start.4 = (f32[81,2048]{1,0:T(8,128)S(1)}, f32[81,2048]{1,0:T(8,128)}, u32[]{:S(2)}) copy-start(f32[81,2048]{1,0:T(8,128)} %param.8) | copy-start | bytes 1990660
  0.7 15.2 %copy-start.3 = (s32[81,2048]{1,0:T(8,128)S(1)}, s32[81,2048]{1,0:T(8,128)}, u32[]{:S(2)}) copy-start(s32[81,2048]{1,0:T(8,128)} %param.9) | copy-start | bytes 1990660
  4.9 64.1 %collective-permute-start.1 = (f32[64,128]{1,0:T(8,128)}, f32[64,128]{1,0:T(8,128)S(1)}, u32[]{:S(2)}, u32[]{:S(2)}) collective-permute-start(f32[64,128]{1,0:T(8,128)} %fusion.51), channel_id=1, source_target_pairs={{1,0},{2,1},{3,2},{4,3},{5,4},{6,5},{7,6},{8,7},{9,8},{10,9},{11,1... | collective-permute-start | bytes 98312 | tf_op jit(solution)/shard_map/ppermute | solution.py:20
  13.3 5.6 copy-start.1
  13.3 55.7 %collective-permute-start = (f32[64,128]{1,0:T(8,128)}, f32[64,128]{1,0:T(8,128)S(1)}, u32[]{:S(2)}, u32[]{:S(2)}) collective-permute-start(f32[64,128]{1,0:T(8,128)} %fusion.65), channel_id=1, source_target_pairs={{0,1},{1,2},{2,3},{3,4},{4,5},{5,6},{6,7},{7,8},{8,9},{9,10},{10,1... | collective-permute-start | bytes 98312 | tf_op jit(solution)/shard_map/ppermute | solution.py:20
  71.9 1.2 copy-start.2
  73.2 0.8 copy-start.6
  73.2 1.4 copy-start.7
  75.2 9.2 %collective-permute-start.2 = (f32[64,128]{1,0:T(8,128)S(1)}, f32[64,128]{1,0:T(8,128)S(1)}, u32[]{:S(2)}, u32[]{:S(2)}) collective-permute-start(f32[64,128]{1,0:T(8,128)S(1)} %fusion.64), channel_id=1, source_target_pairs={{0,1},{1,2},{2,3},{3,4},{4,5},{5,6},{6,7},{7,8},{8,9},{9,10},{10,1... | collective-permute-start | bytes 98312 | tf_op jit(solution)/shard_map/ppermute | solution.py:20
  77.5 8.4 %collective-permute-start.3 = (f32[64,128]{1,0:T(8,128)S(1)}, f32[64,128]{1,0:T(8,128)S(1)}, u32[]{:S(2)}, u32[]{:S(2)}) collective-permute-start(f32[64,128]{1,0:T(8,128)S(1)} %fusion.50), channel_id=1, source_target_pairs={{1,0},{2,1},{3,2},{4,3},{5,4},{6,5},{7,6},{8,7},{9,8},{10,9},{11,1... | collective-permute-start | bytes 98312 | tf_op jit(solution)/shard_map/ppermute | solution.py:20
  90.1 9.7 %collective-permute-start.4 = (f32[64,128]{1,0:T(8,128)S(1)}, f32[64,128]{1,0:T(8,128)S(1)}, u32[]{:S(2)}, u32[]{:S(2)}) collective-permute-start(f32[64,128]{1,0:T(8,128)S(1)} %fusion.63), channel_id=1, source_target_pairs={{0,1},{1,2},{2,3},{3,4},{4,5},{5,6},{6,7},{7,8},{8,9},{9,10},{10,1... | collective-permute-start | bytes 98312 | tf_op jit(solution)/shard_map/ppermute | solution.py:20
  92.0 8.8 %collective-permute-start.5 = (f32[64,128]{1,0:T(8,128)S(1)}, f32[64,128]{1,0:T(8,128)S(1)}, u32[]{:S(2)}, u32[]{:S(2)}) collective-permute-start(f32[64,128]{1,0:T(8,128)S(1)} %fusion.49), channel_id=1, source_target_pairs={{1,0},{2,1},{3,2},{4,3},{5,4},{6,5},{7,6},{8,7},{9,8},{10,9},{11,1... | collective-permute-start | bytes 98312 | tf_op jit(solution)/shard_map/ppermute | solution.py:20
  103.4 0.7 copy-start.5
  267.5 9.3 %collective-permute-start.6 = (f32[64,128]{1,0:T(8,128)S(1)}, f32[64,128]{1,0:T(8,128)S(1)}, u32[]{:S(2)}, u32[]{:S(2)}) collective-permute-start(f32[64,128]{1,0:T(8,128)S(1)} %fusion.62), channel_id=1, source_target_pairs={{0,1},{1,2},{2,3},{3,4},{4,5},{5,6},{6,7},{7,8},{8,9},{9,10},{10,1... | collective-permute-start | bytes 98312 | tf_op jit(solution)/shard_map/ppermute | solution.py:20
  271.1 7.2 %collective-permute-start.7 = (f32[64,128]{1,0:T(8,128)S(1)}, f32[64,128]{1,0:T(8,128)S(1)}, u32[]{:S(2)}, u32[]{:S(2)}) collective-permute-start(f32[64,128]{1,0:T(8,128)S(1)} %fusion.48), channel_id=1, source_target_pairs={{1,0},{2,1},{3,2},{4,3},{5,4},{6,5},{7,6},{8,7},{9,8},{10,9},{11,1... | collective-permute-start | bytes 98312 | tf_op jit(solution)/shard_map/ppermute | solution.py:20
  282.4 9.2 %collective-permute-start.8 = (f32[64,128]{1,0:T(8,128)S(1)}, f32[64,128]{1,0:T(8,128)S(1)}, u32[]{:S(2)}, u32[]{:S(2)}) collective-permute-start(f32[64,128]{1,0:T(8,128)S(1)} %fusion.61), channel_id=1, source_target_pairs={{0,1},{1,2},{2,3},{3,4},{4,5},{5,6},{6,7},{7,8},{8,9},{9,10},{10,1... | collective-permute-start | bytes 98312 | tf_op jit(solution)/shard_map/ppermute | solution.py:20
  284.3 8.8 %collective-permute-start.9 = (f32[64,128]{1,0:T(8,128)S(1)}, f32[64,128]{1,0:T(8,128)S(1)}, u32[]{:S(2)}, u32[]{:S(2)}) collective-permute-start(f32[64,128]{1,0:T(8,128)S(1)} %fusion.47), channel_id=1, source_target_pairs={{1,0},{2,1},{3,2},{4,3},{5,4},{6,5},{7,6},{8,7},{9,8},{10,9},{11,1... | collective-permute-start | bytes 98312 | tf_op jit(solution)/shard_map/ppermute | solution.py:20
  297.2 9.4 %collective-permute-start.10 = (f32[64,128]{1,0:T(8,128)S(1)}, f32[64,128]{1,0:T(8,128)S(1)}, u32[]{:S(2)}, u32[]{:S(2)}) collective-permute-start(f32[64,128]{1,0:T(8,128)S(1)} %fusion.60), channel_id=1, source_target_pairs={{0,1},{1,2},{2,3},{3,4},{4,5},{5,6},{6,7},{7,8},{8,9},{9,10},{10,1... | collective-permute-start | bytes 98312 | tf_op jit(solution)/shard_map/ppermute | solution.py:20
  299.1 8.8 %collective-permute-start.11 = (f32[64,128]{1,0:T(8,128)S(1)}, f32[64,128]{1,0:T(8,128)S(1)}, u32[]{:S(2)}, u32[]{:S(2)}) collective-permute-start(f32[64,128]{1,0:T(8,128)S(1)} %fusion.46), channel_id=1, source_target_pairs={{1,0},{2,1},{3,2},{4,3},{5,4},{6,5},{7,6},{8,7},{9,8},{10,9},{11,1... | collective-permute-start | bytes 98312 | tf_op jit(solution)/shard_map/ppermute | solution.py:20
  312.0 9.2 %collective-permute-start.12 = (f32[64,128]{1,0:T(8,128)S(1)}, f32[64,128]{1,0:T(8,128)S(1)}, u32[]{:S(2)}, u32[]{:S(2)}) collective-permute-start(f32[64,128]{1,0:T(8,128)S(1)} %fusion.59), channel_id=1, source_target_pairs={{0,1},{1,2},{2,3},{3,4},{4,5},{5,6},{6,7},{7,8},{8,9},{9,10},{10,1... | collective-permute-start | bytes 98312 | tf_op jit(solution)/shard_map/ppermute | solution.py:20
  313.9 8.8 %collective-permute-start.13 = (f32[64,128]{1,0:T(8,128)S(1)}, f32[64,128]{1,0:T(8,128)S(1)}, u32[]{:S(2)}, u32[]{:S(2)}) collective-permute-start(f32[64,128]{1,0:T(8,128)S(1)} %fusion.45), channel_id=1, source_target_pairs={{1,0},{2,1},{3,2},{4,3},{5,4},{6,5},{7,6},{8,7},{9,8},{10,9},{11,1... | collective-permute-start | bytes 98312 | tf_op jit(solution)/shard_map/ppermute | solution.py:20
  326.8 9.4 %collective-permute-start.14 = (f32[64,128]{1,0:T(8,128)S(1)}, f32[64,128]{1,0:T(8,128)S(1)}, u32[]{:S(2)}, u32[]{:S(2)}) collective-permute-start(f32[64,128]{1,0:T(8,128)S(1)} %fusion.58), channel_id=1, source_target_pairs={{0,1},{1,2},{2,3},{3,4},{4,5},{5,6},{6,7},{7,8},{8,9},{9,10},{10,1... | collective-permute-start | bytes 98312 | tf_op jit(solution)/shard_map/ppermute | solution.py:20
  328.7 8.8 %collective-permute-start.15 = (f32[64,128]{1,0:T(8,128)S(1)}, f32[64,128]{1,0:T(8,128)S(1)}, u32[]{:S(2)}, u32[]{:S(2)}) collective-permute-start(f32[64,128]{1,0:T(8,128)S(1)} %fusion.44), channel_id=1, source_target_pairs={{1,0},{2,1},{3,2},{4,3},{5,4},{6,5},{7,6},{8,7},{9,8},{10,9},{11,1... | collective-permute-start | bytes 98312 | tf_op jit(solution)/shard_map/ppermute | solution.py:20
  341.7 9.2 %collective-permute-start.16 = (f32[64,128]{1,0:T(8,128)S(1)}, f32[64,128]{1,0:T(8,128)S(1)}, u32[]{:S(2)}, u32[]{:S(2)}) collective-permute-start(f32[64,128]{1,0:T(8,128)S(1)} %fusion.57), channel_id=1, source_target_pairs={{0,1},{1,2},{2,3},{3,4},{4,5},{5,6},{6,7},{7,8},{8,9},{9,10},{10,1... | collective-permute-start | bytes 98312 | tf_op jit(solution)/shard_map/ppermute | solution.py:20
  343.6 8.8 %collective-permute-start.17 = (f32[64,128]{1,0:T(8,128)S(1)}, f32[64,128]{1,0:T(8,128)S(1)}, u32[]{:S(2)}, u32[]{:S(2)}) collective-permute-start(f32[64,128]{1,0:T(8,128)S(1)} %fusion.43), channel_id=1, source_target_pairs={{1,0},{2,1},{3,2},{4,3},{5,4},{6,5},{7,6},{8,7},{9,8},{10,9},{11,1... | collective-permute-start | bytes 98312 | tf_op jit(solution)/shard_map/ppermute | solution.py:20
  356.5 9.7 %collective-permute-start.18 = (f32[64,128]{1,0:T(8,128)S(1)}, f32[64,128]{1,0:T(8,128)S(1)}, u32[]{:S(2)}, u32[]{:S(2)}) collective-permute-start(f32[64,128]{1,0:T(8,128)S(1)} %fusion.56), channel_id=1, source_target_pairs={{0,1},{1,2},{2,3},{3,4},{4,5},{5,6},{6,7},{7,8},{8,9},{9,10},{10,1... | collective-permute-start | bytes 98312 | tf_op jit(solution)/shard_map/ppermute | solution.py:20
  358.4 8.8 %collective-permute-start.19 = (f32[64,128]{1,0:T(8,128)S(1)}, f32[64,128]{1,0:T(8,128)S(1)}, u32[]{:S(2)}, u32[]{:S(2)}) collective-permute-start(f32[64,128]{1,0:T(8,128)S(1)} %fusion.42), channel_id=1, source_target_pairs={{1,0},{2,1},{3,2},{4,3},{5,4},{6,5},{7,6},{8,7},{9,8},{10,9},{11,1... | collective-permute-start | bytes 98312 | tf_op jit(solution)/shard_map/ppermute | solution.py:20
  533.6 9.3 %collective-permute-start.20 = (f32[64,128]{1,0:T(8,128)S(1)}, f32[64,128]{1,0:T(8,128)S(1)}, u32[]{:S(2)}, u32[]{:S(2)}) collective-permute-start(f32[64,128]{1,0:T(8,128)S(1)} %fusion.55), channel_id=1, source_target_pairs={{0,1},{1,2},{2,3},{3,4},{4,5},{5,6},{6,7},{7,8},{8,9},{9,10},{10,1... | collective-permute-start | bytes 98312 | tf_op jit(solution)/shard_map/ppermute | solution.py:20
  535.5 8.8 %collective-permute-start.21 = (f32[64,128]{1,0:T(8,128)S(1)}, f32[64,128]{1,0:T(8,128)S(1)}, u32[]{:S(2)}, u32[]{:S(2)}) collective-permute-start(f32[64,128]{1,0:T(8,128)S(1)} %fusion.41), channel_id=1, source_target_pairs={{1,0},{2,1},{3,2},{4,3},{5,4},{6,5},{7,6},{8,7},{9,8},{10,9},{11,1... | collective-permute-start | bytes 98312 | tf_op jit(solution)/shard_map/ppermute | solution.py:20
  548.4 9.2 %collective-permute-start.22 = (f32[64,128]{1,0:T(8,128)S(1)}, f32[64,128]{1,0:T(8,128)S(1)}, u32[]{:S(2)}, u32[]{:S(2)}) collective-permute-start(f32[64,128]{1,0:T(8,128)S(1)} %fusion.54), channel_id=1, source_target_pairs={{0,1},{1,2},{2,3},{3,4},{4,5},{5,6},{6,7},{7,8},{8,9},{9,10},{10,1... | collective-permute-start | bytes 98312 | tf_op jit(solution)/shard_map/ppermute | solution.py:20
  550.3 8.8 %collective-permute-start.23 = (f32[64,128]{1,0:T(8,128)S(1)}, f32[64,128]{1,0:T(8,128)S(1)}, u32[]{:S(2)}, u32[]{:S(2)}) collective-permute-start(f32[64,128]{1,0:T(8,128)S(1)} %fusion.40), channel_id=1, source_target_pairs={{1,0},{2,1},{3,2},{4,3},{5,4},{6,5},{7,6},{8,7},{9,8},{10,9},{11,1... | collective-permute-start | bytes 98312 | tf_op jit(solution)/shard_map/ppermute | solution.py:20
  563.2 9.5 %collective-permute-start.24 = (f32[64,128]{1,0:T(8,128)S(1)}, f32[64,128]{1,0:T(8,128)S(1)}, u32[]{:S(2)}, u32[]{:S(2)}) collective-permute-start(f32[64,128]{1,0:T(8,128)S(1)} %fusion.53), channel_id=1, source_target_pairs={{0,1},{1,2},{2,3},{3,4},{4,5},{5,6},{6,7},{7,8},{8,9},{9,10},{10,1... | collective-permute-start | bytes 98312 | tf_op jit(solution)/shard_map/ppermute | solution.py:20
  565.2 8.9 %collective-permute-start.25 = (f32[64,128]{1,0:T(8,128)S(1)}, f32[64,128]{1,0:T(8,128)S(1)}, u32[]{:S(2)}, u32[]{:S(2)}) collective-permute-start(f32[64,128]{1,0:T(8,128)S(1)} %fusion.39), channel_id=1, source_target_pairs={{1,0},{2,1},{3,2},{4,3},{5,4},{6,5},{7,6},{8,7},{9,8},{10,9},{11,1... | collective-permute-start | bytes 98312 | tf_op jit(solution)/shard_map/ppermute | solution.py:20
  579.6 9.2 %collective-permute-start.26 = (f32[64,128]{1,0:T(8,128)S(1)}, f32[64,128]{1,0:T(8,128)S(1)}, u32[]{:S(2)}, u32[]{:S(2)}) collective-permute-start(f32[64,128]{1,0:T(8,128)S(1)} %fusion.52), channel_id=1, source_target_pairs={{0,1},{1,2},{2,3},{3,4},{4,5},{5,6},{6,7},{7,8},{8,9},{9,10},{10,1... | collective-permute-start | bytes 98312 | tf_op jit(solution)/shard_map/ppermute | solution.py:20
  581.6 8.8 %collective-permute-start.27 = (f32[64,128]{1,0:T(8,128)S(1)}, f32[64,128]{1,0:T(8,128)S(1)}, u32[]{:S(2)}, u32[]{:S(2)}) collective-permute-start(f32[64,128]{1,0:T(8,128)S(1)} %fusion.38), channel_id=1, source_target_pairs={{1,0},{2,1},{3,2},{4,3},{5,4},{6,5},{7,6},{8,7},{9,8},{10,9},{11,1... | collective-permute-start | bytes 98312 | tf_op jit(solution)/shard_map/ppermute | solution.py:20
where the time goes:
time: 600 us; the launch traced here: 594 us
  blocking collectives  314 us (52%)
  starting transfers between devices  129 us (22%)
  matrix products  64.9 us (11%)
  other arithmetic  61.1 us (10%)
  waiting for transfers between devices  18.4 us (3%)
    all_gather x10, blocking collectives, apply_coarse(): whole = lax.all_gather(vector, 'sub', axis=0, tiled=True)  314 us
    ppermute x28, starting transfers between devices, from_behind(): return lax.ppermute(shard, axis, pairs)  129 us
    add x1, other arithmetic, band_tiles(): tiles + jnp.where(local[entry][:, None] == places, fine_values[entry][:,...  47.5 us
    ppermute x28, waiting for transfers between devices, from_behind(): return lax.ppermute(shard, axis, pairs)  18.4 us
    dot_general x14, matrix products, fine_apply(): jnp.einsum('brc,bcn->brn', low_tiles, pieces[:-1], precision=highest)  17.3 us
    dot_general x14, matrix products, fine_apply(): jnp.einsum('brc,bcn->brn', high_tiles, pieces[1:], precision=highest)  16.8 us
  transfers between devices with their start and end apart: 28, of which 13 were waited for; matrix products, arithmetic and copies ran while one was open for 9% of the time, Pallas kernels for 0%

commit v1 on v0

v1 whole, which is shorter than its diff:
```python
import functools

import jax
import jax.numpy as jnp
from jax import lax
from jax.experimental import pallas as pl
from jax.experimental.pallas import tpu as pltpu
from jax.sharding import PartitionSpec as P

CHEB_FINE = 2
CHEB_COARSE = 6
CYCLES = 2
APPLIES = 7

THETA = 1.0
DELTA = 0.7
OMEGA = 0.6
MESH = pl.DeviceIdType.MESH
f32 = jnp.float32
bf16 = jnp.bfloat16


def split(x):
    hi = x.astype(bf16)
    lo = (x - hi.astype(f32)).astype(bf16)
    return hi, lo


def iota(shape, dim):
    return lax.broadcasted_iota(jnp.int32, shape, dim)


def setup_kernel(fv_ref, col_ref, agg_ref, a_ref, dinv_ref, diag_ref, oht_ref, oh_ref):
    block = fv_ref.shape[1]
    count = fv_ref.shape[0] - 1
    groups = count // 8
    base = pl.program_id(0) * block
    rows = iota((8, block), 1)
    cols, vals, firsts = [], [], []
    for i in range(groups):
        cols.append(col_ref[1 + 8 * i : 9 + 8 * i, :] - base - rows)
        vals.append(fv_ref[1 + 8 * i : 9 + 8 * i, :])
    last = jnp.zeros((8, block), f32)
    for i in range(groups):
        last = last + jnp.where(cols[i] == block, vals[i], 0.0)
    last = jnp.sum(last, axis=0, keepdims=True)
    for j in range(groups):
        total = vals[j]
        for i in range(j + 1, groups):
            total = total + jnp.where(cols[i] == cols[j], vals[i], 0.0)
        firsts.append(total)
    high_count = block // 8
    places = [iota((8, block), 0) + 8 * h for h in range(high_count)]
    sums = [jnp.zeros((8, block), f32)] * high_count
    for s in range(8):
        chains = [jnp.zeros((8, block), f32)] * high_count
        for i in reversed(range(groups)):
            col = jnp.broadcast_to(cols[i][s : s + 1, :], (8, block))
            val = jnp.broadcast_to(firsts[i][s : s + 1, :], (8, block))
            chains = [jnp.where(col == places[h], val, chains[h]) for h in range(high_count)]
        sums = [sums[h] + chains[h] for h in range(high_count)]
    by_offset = jnp.concatenate(sums, axis=0).T
    skewed = pltpu.roll(by_offset, 0, 1, stride=1, stride_axis=0)
    lane = iota((block, block), 1)
    sub = iota((block, block), 0)
    low = jnp.where(lane >= sub, skewed, 0.0)
    high = jnp.where(lane < sub, skewed, jnp.where(lane == sub, last, 0.0))
    for part, at in ((low, 0), (high, block)):
        hi, lo = split(part)
        a_ref[:block, at : at + block] = hi
        a_ref[block:, at : at + block] = lo
    diag = jnp.broadcast_to(fv_ref[0:1, :], (block, block)).T
    diag_ref[...] = diag
    dinv_ref[...] = 1.0 / diag
    count_agg = oht_ref.shape[0]
    onehot = (iota((count_agg, block), 0) == agg_ref[...]).astype(f32)
    oht_ref[...] = onehot.astype(bf16)
    oh_ref[...] = onehot.T.astype(bf16)


def run_setup(fine_values, columns, agg_map, block, aggregates):
    entries, rows = fine_values.shape
    blocks = rows // block
    return pl.pallas_call(
        setup_kernel,
        grid=(blocks,),
        in_specs=[
            pl.BlockSpec((entries, block), lambda b: (0, b)),
            pl.BlockSpec((entries, block), lambda b: (0, b)),
            pl.BlockSpec((1, block), lambda b: (0, b)),
        ],
        out_specs=[
            pl.BlockSpec((2 * block, 2 * block), lambda b: (b, 0)),
            pl.BlockSpec((block, block), lambda b: (b, 0)),
            pl.BlockSpec((block, block), lambda b: (b, 0)),
            pl.BlockSpec((aggregates, block), lambda b: (0, b)),
            pl.BlockSpec((block, aggregates), lambda b: (b, 0)),
        ],
        out_shape=[
            jax.ShapeDtypeStruct((2 * rows, 2 * block), bf16),
            jax.ShapeDtypeStruct((rows, block), f32),
            jax.ShapeDtypeStruct((rows, block), f32),
            jax.ShapeDtypeStruct((aggregates, rows), bf16),
            jax.ShapeDtypeStruct((rows, aggregates), bf16),
        ],
        name="setup",
    )(fine_values, columns, agg_map.reshape(1, rows))


def quads(product, rows, width):
    return product[:rows, :width] + (product[:rows, width:] + product[rows:, :width])


def main_kernel(
    n_grp, n_sub,
    rhs_ref, a_ref, dinv_ref, diag_ref, oht_ref, oh_ref, lo_ref, hi_ref, coarse_ref,
    sol_ref, res_ref,
    xs, ext, s2, m2, send, recv, csend, whole, send_sem, recv_sem, csend_sem, crecv_sem,
):
    rows_dev, width = rhs_ref.shape
    ghost = lo_ref.shape[0]
    block = 2 * ghost
    blocks = rows_dev // block
    agg = coarse_ref.shape[0]
    grp = lax.axis_index("grp")
    me = lax.axis_index("sub")
    part = grp * n_sub + me
    has_next = part < n_grp * n_sub - 1
    has_prev = part > 0
    after, before = part + 1, part - 1
    next_id = (lax.div(after, n_sub), lax.rem(after, n_sub))
    prev_id = (lax.div(before, n_sub), lax.rem(before, n_sub))
    cross_next = jnp.logical_and(has_next, me == n_sub - 1)
    cross_prev = jnp.logical_and(has_prev, me == 0)

    barrier = pltpu.get_barrier_semaphore()
    for j in range(1, n_sub):
        pl.semaphore_signal(barrier, inc=1, device_id=(grp, lax.rem(me + j, n_sub)), device_id_type=MESH)

    @pl.when(cross_next)
    def _():
        pl.semaphore_signal(barrier, inc=1, device_id=next_id, device_id_type=MESH)

    @pl.when(cross_prev)
    def _():
        pl.semaphore_signal(barrier, inc=1, device_id=prev_id, device_id_type=MESH)

    own = coarse_ref[...]
    hi, lo = split(own)
    m2[:agg, :] = hi
    m2[agg:, :] = lo
    mine = pl.multiple_of(me * agg, agg)
    center = coarse_ref[:, pl.ds(mine, agg)]
    eye = iota((agg, agg), 0) == iota((agg, agg), 1)
    cinv = 1.0 / jnp.sum(jnp.where(eye, center, 0.0), axis=1, keepdims=True)
    cinv = jnp.broadcast_to(cinv, (agg, width))
    ext[:ghost, :] = jnp.zeros((ghost, 2 * width), bf16)
    ext[ghost + rows_dev :, :] = jnp.zeros((ghost, 2 * width), bf16)

    def each_block(fn):
        def go(b, carry):
            fn(pl.ds(pl.multiple_of(b * block, block), block))
            return carry
        lax.fori_loop(0, blocks, go, 0, unroll=True)

    def first(sl):
        rhs = rhs_ref[sl, :]
        res_ref[sl, :] = rhs
        sol_ref[sl, :] = jnp.zeros_like(rhs)
        xs[0, sl, :] = dinv_ref[sl, :] * rhs

    each_block(first)
    pl.semaphore_wait(barrier, n_sub - 1 + cross_next.astype(jnp.int32) + cross_prev.astype(jnp.int32))

    def halo_copy(ex, way, device):
        return pltpu.make_async_remote_copy(
            src_ref=send.at[ex, way], dst_ref=recv.at[ex, way],
            send_sem=send_sem.at[ex, way], recv_sem=recv_sem.at[ex, way],
            device_id=device, device_id_type=MESH,
        )

    def apply(ex, cur, epilogue):
        up = halo_copy(ex, 0, next_id)
        down = halo_copy(ex, 1, prev_id)

        @pl.when(has_next)
        def _():
            for i in range(ghost):
                send[ex, 0, i : i + 1, :] = xs[cur, pl.ds(hi_ref[i], 1), :]
            up.start()

        @pl.when(has_prev)
        def _():
            for i in range(ghost):
                send[ex, 1, i : i + 1, :] = xs[cur, pl.ds(lo_ref[i], 1), :]
            down.start()

        for b in range(blocks):
            hi, lo = split(xs[cur, b * block : (b + 1) * block, :])
            at = ghost + b * block
            ext[at : at + block, :width] = hi
            ext[at : at + block, width:] = lo

        def one(b):
            a = a_ref[pl.ds(pl.multiple_of(b * 2 * block, 2 * block), 2 * block), :]
            x = ext[pl.ds(pl.multiple_of(b * block, block), 2 * block), :]
            off = quads(jnp.dot(a, x, preferred_element_type=f32), block, width)
            epilogue(pl.ds(pl.multiple_of(b * block, block), block), off)

        def go(b, carry):
            one(1 + 2 * b)
            one(2 + 2 * b)
            return carry

        lax.fori_loop(0, (blocks - 2) // 2, go, 0)

        @pl.when(has_next)
        def _():
            down.wait_recv()
            hi, lo = split(recv[ex, 1])
            ext[ghost + rows_dev :, :width] = hi
            ext[ghost + rows_dev :, width:] = lo
            up.wait_send()

        @pl.when(has_prev)
        def _():
            up.wait_recv()
            hi, lo = split(recv[ex, 0])
            ext[:ghost, :width] = hi
            ext[:ghost, width:] = lo
            down.wait_send()

        one(0)
        one(blocks - 1)

    def gather(step, value):
        csend[step] = value
        copies = []
        for j in range(1, n_sub):
            copies.append(pltpu.make_async_remote_copy(
                src_ref=csend.at[step], dst_ref=whole.at[step, pl.ds(mine, agg)],
                send_sem=csend_sem.at[step, j], recv_sem=crecv_sem.at[step, j],
                device_id=(grp, lax.rem(me + j, n_sub)), device_id_type=MESH,
            ))
        for copy in copies:
            copy.start()
        whole[step, pl.ds(mine, agg), :] = value
        for copy in copies:
            copy.wait()
        hi, lo = split(whole[step])
        x = jnp.concatenate([hi, lo], axis=1)
        return quads(jnp.dot(m2[...], x, preferred_element_type=f32), agg, width)

    rho0 = DELTA / THETA
    rho1 = 1.0 / (2.0 * THETA / DELTA - rho0)
    c1 = rho1 * rho0
    c2 = 2.0 * rho1 / DELTA

    def smooth(ex):
        def step_one(sl, off):
            d0 = xs[0, sl, :]
            r0 = res_ref[sl, :]
            d1 = c1 * d0 - c2 * dinv_ref[sl, :] * off
            xs[1, sl, :] = d1
            res_ref[sl, :] = (c2 - 1.0) * off - c1 * r0
            sol_ref[sl, :] += d0 + d1

        apply(ex, 0, step_one)

        def step_two(sl, off):
            r = res_ref[sl, :] - off
            res_ref[sl, :] = r
            xs[0, sl, :] = dinv_ref[sl, :] * r

        apply(ex + 1, 1, step_two)

    def cycle_body(cycle, carry):
        ex = cycle * APPLIES
        smooth(ex)

        def restrict(sl, off):
            s = (1.0 - OMEGA) * res_ref[sl, :] - OMEGA * off
            hi, lo = split(s)
            s2[sl, :width] = hi
            s2[sl, width:] = lo

        apply(ex + 2, 0, restrict)
        both = jnp.dot(oht_ref[...], s2[...], preferred_element_type=f32)
        r = both[:, :width] + both[:, width:]
        d = cinv * r
        result = d
        rho_old = rho0
        for turn in range(1, CHEB_COARSE):
            r = r - gather(cycle * (CHEB_COARSE - 1) + turn - 1, d)
            rho_new = 1.0 / (2.0 * THETA / DELTA - rho_old)
            d = rho_new * rho_old * d + (2.0 * rho_new / DELTA) * (cinv * r)
            result = result + d
            rho_old = rho_new
        hi, lo = split(result)
        packed = jnp.concatenate([hi, lo], axis=1)

        def spread(sl):
            both = jnp.dot(oh_ref[sl, :], packed, preferred_element_type=f32)
            xs[0, sl, :] = both[:, :width] + both[:, width:]

        each_block(spread)

        def prolong(sl, off):
            e = (1.0 - OMEGA) * xs[0, sl, :] - OMEGA * (dinv_ref[sl, :] * off)
            xs[1, sl, :] = e
            sol_ref[sl, :] += e

        apply(ex + 3, 0, prolong)

        def correct(sl, off):
            r = res_ref[sl, :] - (diag_ref[sl, :] * xs[1, sl, :] + off)
            res_ref[sl, :] = r
            xs[0, sl, :] = dinv_ref[sl, :] * r

        apply(ex + 4, 1, correct)
        smooth(ex + 5)
        return carry

    lax.fori_loop(0, CYCLES, cycle_body, 0)


def body(n_grp, n_sub, right_side, fine_values, columns, agg_map, send_lo, send_hi, coarse_matrix):
    rows, width = right_side.shape
    ghost = send_lo.shape[0]
    block = 2 * ghost
    own = coarse_matrix[0]
    agg, coarse = own.shape
    a2, dinv, diag, oht, oh = run_setup(fine_values, columns, agg_map, block, agg)
    exchanges = CYCLES * APPLIES
    gathers = CYCLES * (CHEB_COARSE - 1)
    vmem = pl.BlockSpec(memory_space=pltpu.VMEM)
    smem = pl.BlockSpec(memory_space=pltpu.SMEM)
    return pl.pallas_call(
        functools.partial(main_kernel, n_grp, n_sub),
        in_specs=[vmem] * 6 + [smem] * 2 + [vmem],
        out_specs=[vmem] * 2,
        out_shape=[jax.ShapeDtypeStruct((rows, width), f32)] * 2,
        scratch_shapes=[
            pltpu.VMEM((2, rows, width), f32),
            pltpu.VMEM((rows + block, 2 * width), bf16),
            pltpu.VMEM((rows, 2 * width), bf16),
            pltpu.VMEM((2 * agg, coarse), bf16),
            pltpu.VMEM((exchanges, 2, ghost, width), f32),
            pltpu.VMEM((exchanges, 2, ghost, width), f32),
            pltpu.VMEM((gathers, agg, width), f32),
            pltpu.VMEM((gathers, coarse, width), f32),
            pltpu.SemaphoreType.DMA((exchanges, 2)),
            pltpu.SemaphoreType.DMA((exchanges, 2)),
            pltpu.SemaphoreType.DMA((gathers, n_sub)),
            pltpu.SemaphoreType.DMA((gathers, n_sub)),
        ],
        compiler_params=pltpu.CompilerParams(
            collective_id=0, has_side_effects=True, vmem_limit_bytes=50 * 1024 * 1024
        ),
        name="cycles",
    )(right_side, a2, dinv, diag, oht, oh, send_lo, send_hi, own)


def solution(mesh):
    placed = (
        P(("grp", "sub"), None),
        P(None, ("grp", "sub")),
        P(None, ("grp", "sub")),
        P(("grp", "sub")),
        P(("grp", "sub")),
        P(("grp", "sub")),
        P("grp", "sub", None),
    )
    return jax.shard_map(
        functools.partial(body, mesh.shape["grp"], mesh.shape["sub"]),
        mesh=mesh,
        in_specs=placed,
        out_specs=(P(("grp", "sub"), None), P(("grp", "sub"), None)),
        check_vma=False,
    )
```

time: 600 us -> 219 us (0.36)
  blocking collectives: 314 us -> 0 us
  Pallas kernels: 0 us -> 210 us
  starting transfers between devices: 129 us -> 0 us
  matrix products: 64.9 us -> 0 us
  other arithmetic: 61.1 us -> 0 us
  waiting for transfers between devices: 18.4 us -> 0 us
    all_gather x10 -> x0, blocking collectives: 314 us -> none  [apply_coarse(): whole = lax.all_gather(vector, 'sub', axis=0, tiled=True)]
    pallas_call x0 -> x2, Pallas kernels: none -> 210 us  [the longest x1 196 us: body(): pl.pallas_call(functools.partial(main_kernel, n_grp, n_sub), in_specs=[vm...]
    ppermute x28 -> x0, starting transfers between devices: 129 us -> none  [from_behind(): return lax.ppermute(shard, axis, pairs)]
    dot_general x70 -> x0, matrix products: 64.9 us -> none  [the longest x14 17.3 us: fine_apply(): jnp.einsum('brc,bcn->brn', low_tiles, pieces[:-1], precision=highest)]
    add x5 -> x0, other arithmetic: 50.7 us -> none  [the longest x1 47.5 us: band_tiles(): tiles + jnp.where(local[entry][:, None] == places, fine_values[entry][:,...]
    ppermute x28 -> x0, waiting for transfers between devices: 18.4 us -> none  [from_behind(): return lax.ppermute(shard, axis, pairs)]
  transfers between devices with their start and end apart: 28 -> 0, of which waited for: 13 -> 0; matrix products, arithmetic and copies ran while one was open for 9% -> 0% of each run, Pallas kernels for 0% -> 0%
where the time goes in v1:
time: 219 us; the launch traced here: 218 us
  Pallas kernels  210 us (96%)
  local copies, waits for them, and re-layouts  6.37 us (3%)
    pallas_call x1, Pallas kernels, body(): pl.pallas_call(functools.partial(main_kernel, n_grp, n_sub), in_specs=[vm...  196 us
    pallas_call x1, Pallas kernels, run_setup(): pl.pallas_call(setup_kernel, grid=(blocks,), in_specs=[pl.BlockSpec((entr...  14.2 us
    unnamed x12, local copies, waits for them, and re-layouts  6.37 us

profile of v1, /device:TPU:2, one launch (start us, length us, event | category | flops | bytes accessed | tf_op | source)
XLA Modules:
  0.0 217.5 jit_solution(11166914281629900397)
XLA Ops:
  0.6 14.2 %setup.1 = (bf16[4096,256]{1,0:T(8,128)(2,1)}, f32[2048,128]{1,0:T(8,128)}, f32[2048,128]{1,0:T(8,128)}, bf16[128,2048]{1,0:T(8,128)(2,1)}, bf16[2048,128]{1,0:T(8,128)(2,1)}) custom-call(f32[81,2048]{1,0:T(8,128)} %fv_ref.1, s32[81,2048]{1,0:T(8,128)} %col_ref.1, s32[1,2048]{1,0:T(1,128)} %bitcast.3), custom_call_target="tpu_custom_call" | custom-call | tf_op jit(solution)/shard_map/setup/pallas_call | solution.py:84
  14.9 0.0 copy-start
  14.9 1.0 copy-done
  15.9 0.0 copy-start.1
  15.9 1.0 copy-done.1
  16.9 0.0 copy-start.2
  16.9 1.0 copy-done.2
  18.0 0.0 copy-start.3
  18.0 0.7 copy-done.3
  18.6 0.0 copy-start.4
  18.6 0.7 copy-done.4
  19.3 196.3 %cycles.1 = (f32[2048,128]{1,0:T(8,128)S(1)}, f32[2048,128]{1,0:T(8,128)S(1)}) custom-call(f32[2048,128]{1,0:T(8,128)} %rhs_ref.1, bf16[4096,256]{1,0:T(8,128)(2,1)} %get-tuple-element.7.a_ref, f32[2048,128]{1,0:T(8,128)} %get-tuple-element.8.dinv_ref, f32[2048,128]{1,0:T(8,128)} %get-tuple-element.9.diag_ref, bf16[128,2048]{1,0:T(8,128)(2,1)S(1)} %copy-done.1, ...), custom_call_target="tpu_custom_call" | custom-call | tf_op jit(solution)/shard_map/cycles/pallas_call | solution.py:338
  215.6 1.0 copy.11
  216.6 1.0 copy.12
Async XLA Ops:
  14.9 1.0 copy-start
  15.9 1.0 copy-start.1
  16.9 1.0 copy-start.2
  18.0 0.7 copy-start.3
  18.6 0.7 copy-start.4

commit v2 on v1

--- a/solution.py
+++ b/solution.py
@@ -103,25 +103,98 @@
             jax.ShapeDtypeStruct((aggregates, rows), bf16),
             jax.ShapeDtypeStruct((rows, aggregates), bf16),
         ],
+        cost_estimate=pl.CostEstimate(flops=10_000_000_000, bytes_accessed=50_000_000, transcendentals=0),
         name="setup",
     )(fine_values, columns, agg_map.reshape(1, rows))
 
 
+def poly_kernel(m_ref, out_ref, m_hi, m_lo, d_ref, z_ref, x_ref, pair):
+    coarse = m_ref.shape[0]
+    agg = x_ref.shape[0]
+    parts = coarse // agg
+    half = parts // 2
+    me = lax.axis_index("sub")
+    eye = iota((agg, agg), 0) == iota((agg, agg), 1)
+    cinv = []
+    for j in range(coarse // agg):
+        sl = slice(j * agg, (j + 1) * agg)
+        cinv.append(1.0 / jnp.sum(jnp.where(eye, m_ref[sl, :agg], 0.0), axis=0, keepdims=True))
+        for k in range(half + 1):
+            other = (j + k) % parts
+            so = slice(other * agg, (other + 1) * agg)
+            tile = m_ref[sl, k * agg : (k + 1) * agg]
+            m_hi[sl, so], m_lo[sl, so] = split(tile)
+            if 0 < k and 2 * k < parts:
+                m_hi[so, sl], m_lo[so, sl] = split(tile.T)
+    for j in range(coarse // agg):
+        sl = slice(j * agg, (j + 1) * agg)
+        start = jnp.where(jnp.logical_and(eye, me == j), cinv[j], 0.0)
+        d_ref[:, sl] = start
+        z_ref[:, sl] = start
+        x_ref[:, sl] = start
+    rho_old = DELTA / THETA
+    for turn in range(1, CHEB_COARSE):
+        rho_new = 1.0 / (2.0 * THETA / DELTA - rho_old)
+        hi, lo = split(d_ref[...])
+        pair[:agg, :] = hi
+        pair[agg:, :] = lo
+        for j in range(coarse // agg // 2):
+            sl = slice(2 * j * agg, (2 * j + 2) * agg)
+            both = jnp.dot(pair[...], m_hi[:, sl], preferred_element_type=f32)
+            low = jnp.dot(pair[:agg, :], m_lo[:, sl], preferred_element_type=f32)
+            scale = jnp.concatenate([cinv[2 * j], cinv[2 * j + 1]], axis=1)
+            z = z_ref[:, sl] - (both[:agg] + (both[agg:] + low)) * scale
+            d = rho_new * rho_old * d_ref[:, sl] + (2.0 * rho_new / DELTA) * z
+            z_ref[:, sl] = z
+            d_ref[:, sl] = d
+            x_ref[:, sl] += d
+        rho_old = rho_new
+    hi, lo = split(x_ref[...])
+    out_ref[:agg, :] = hi
+    out_ref[agg:, :] = lo
+
+
+def run_poly(matrix, agg):
+    coarse = matrix.shape[0]
+    vmem = pl.BlockSpec(memory_space=pltpu.VMEM)
+    return pl.pallas_call(
+        poly_kernel,
+        in_specs=[vmem],
+        out_specs=vmem,
+        out_shape=jax.ShapeDtypeStruct((2 * agg, coarse), bf16),
+        scratch_shapes=[
+            pltpu.VMEM((coarse, coarse), bf16),
+            pltpu.VMEM((coarse, coarse), bf16),
+            pltpu.VMEM((agg, coarse), f32),
+            pltpu.VMEM((agg, coarse), f32),
+            pltpu.VMEM((agg, coarse), f32),
+            pltpu.VMEM((2 * agg, coarse), bf16),
+        ],
+        compiler_params=pltpu.CompilerParams(vmem_limit_bytes=50 * 1024 * 1024),
+        name="poly",
+    )(matrix)
+
+
 def quads(product, rows, width):
     return product[:rows, :width] + (product[:rows, width:] + product[rows:, :width])
 
 
-def main_kernel(
-    n_grp, n_sub,
-    rhs_ref, a_ref, dinv_ref, diag_ref, oht_ref, oh_ref, lo_ref, hi_ref, coarse_ref,
-    sol_ref, res_ref,
-    xs, ext, s2, m2, send, recv, csend, whole, send_sem, recv_sem, csend_sem, crecv_sem,
-):
+def main_kernel(opening, n_grp, n_sub, *refs):
+    if opening:
+        (rhs_ref, a_ref, dinv_ref, oht_ref, lo_ref, hi_ref,
+         sol_ref, res_ref, crhs_ref,
+         xs, ext, s2, send, recv, send_sem, recv_sem) = refs
+        agg = oht_ref.shape[0]
+    else:
+        (sol_in, rhs_ref, crhs_ref, a_ref, dinv_ref, diag_ref, oht_ref, oh_ref, lo_ref, hi_ref, m2,
+         sol_ref, res_ref,
+         xs, ext, s2, send, recv, send_sem, recv_sem,
+         csend, whole, csend_sem, crecv_sem) = refs
+        agg = oht_ref.shape[0]
     rows_dev, width = rhs_ref.shape
     ghost = lo_ref.shape[0]
     block = 2 * ghost
     blocks = rows_dev // block
-    agg = coarse_ref.shape[0]
     grp = lax.axis_index("grp")
     me = lax.axis_index("sub")
     part = grp * n_sub + me
@@ -134,26 +207,22 @@
     cross_prev = jnp.logical_and(has_prev, me == 0)
 
     barrier = pltpu.get_barrier_semaphore()
-    for j in range(1, n_sub):
-        pl.semaphore_signal(barrier, inc=1, device_id=(grp, lax.rem(me + j, n_sub)), device_id_type=MESH)
-
-    @pl.when(cross_next)
+    if opening:
+        greet_next, greet_prev, greeted = has_next, has_prev, 0
+    else:
+        greet_next, greet_prev, greeted = cross_next, cross_prev, n_sub - 1
+        for j in range(1, n_sub):
+            pl.semaphore_signal(barrier, inc=1, device_id=(grp, lax.rem(me + j, n_sub)), device_id_type=MESH)
+
+    @pl.when(greet_next)
     def _():
         pl.semaphore_signal(barrier, inc=1, device_id=next_id, device_id_type=MESH)
 
-    @pl.when(cross_prev)
+    @pl.when(greet_prev)
     def _():
         pl.semaphore_signal(barrier, inc=1, device_id=prev_id, device_id_type=MESH)
 
-    own = coarse_ref[...]
-    hi, lo = split(own)
-    m2[:agg, :] = hi
-    m2[agg:, :] = lo
     mine = pl.multiple_of(me * agg, agg)
-    center = coarse_ref[:, pl.ds(mine, agg)]
-    eye = iota((agg, agg), 0) == iota((agg, agg), 1)
-    cinv = 1.0 / jnp.sum(jnp.where(eye, center, 0.0), axis=1, keepdims=True)
-    cinv = jnp.broadcast_to(cinv, (agg, width))
     ext[:ghost, :] = jnp.zeros((ghost, 2 * width), bf16)
     ext[ghost + rows_dev :, :] = jnp.zeros((ghost, 2 * width), bf16)
 
@@ -166,11 +235,14 @@
     def first(sl):
         rhs = rhs_ref[sl, :]
         res_ref[sl, :] = rhs
-        sol_ref[sl, :] = jnp.zeros_like(rhs)
-        xs[0, sl, :] = dinv_ref[sl, :] * rhs
+        if opening:
+            sol_ref[sl, :] = jnp.zeros_like(rhs)
+            xs[0, sl, :] = dinv_ref[sl, :] * rhs
+        else:
+            sol_ref[sl, :] = sol_in[sl, :]
 
     each_block(first)
-    pl.semaphore_wait(barrier, n_sub - 1 + cross_next.astype(jnp.int32) + cross_prev.astype(jnp.int32))
+    pl.semaphore_wait(barrier, greeted + greet_next.astype(jnp.int32) + greet_prev.astype(jnp.int32))
 
     def halo_copy(ex, way, device):
         return pltpu.make_async_remote_copy(
@@ -185,14 +257,22 @@
 
         @pl.when(has_next)
         def _():
-            for i in range(ghost):
-                send[ex, 0, i : i + 1, :] = xs[cur, pl.ds(hi_ref[i], 1), :]
+            def pick(i, carry):
+                for k in range(16):
+                    send[ex, 0, pl.ds(16 * i + k, 1), :] = xs[cur, pl.ds(hi_ref[16 * i + k], 1), :]
+                return carry
+
+            lax.fori_loop(0, ghost // 16, pick, 0)
             up.start()
 
         @pl.when(has_prev)
         def _():
-            for i in range(ghost):
-                send[ex, 1, i : i + 1, :] = xs[cur, pl.ds(lo_ref[i], 1), :]
+            def pick(i, carry):
+                for k in range(16):
+                    send[ex, 1, pl.ds(16 * i + k, 1), :] = xs[cur, pl.ds(lo_ref[16 * i + k], 1), :]
+                return carry
+
+            lax.fori_loop(0, ghost // 16, pick, 0)
             down.start()
 
         for b in range(blocks):
@@ -233,8 +313,7 @@
         one(0)
         one(blocks - 1)
 
-    def gather(step, value):
-        csend[step] = value
+    def gather(step):
         copies = []
         for j in range(1, n_sub):
             copies.append(pltpu.make_async_remote_copy(
@@ -244,7 +323,7 @@
             ))
         for copy in copies:
             copy.start()
-        whole[step, pl.ds(mine, agg), :] = value
+        whole[step, pl.ds(mine, agg), :] = csend[step]
         for copy in copies:
             copy.wait()
         hi, lo = split(whole[step])
@@ -274,29 +353,27 @@
 
         apply(ex + 1, 1, step_two)
 
+    def restrict(sl, off):
+        s = (1.0 - OMEGA) * res_ref[sl, :] - OMEGA * off
+        hi, lo = split(s)
+        s2[sl, :width] = hi
+        s2[sl, width:] = lo
+
+    def restricted(ex):
+        apply(ex, 0, restrict)
+        both = jnp.dot(oht_ref[...], s2[...], preferred_element_type=f32)
+        return both[:, :width] + both[:, width:]
+
+    if opening:
+        smooth(0)
+        crhs_ref[...] = restricted(2)
+        return
+
+    csend[0] = crhs_ref[...]
+
     def cycle_body(cycle, carry):
         ex = cycle * APPLIES
-        smooth(ex)
-
-        def restrict(sl, off):
-            s = (1.0 - OMEGA) * res_ref[sl, :] - OMEGA * off
-            hi, lo = split(s)
-            s2[sl, :width] = hi
-            s2[sl, width:] = lo
-
-        apply(ex + 2, 0, restrict)
-        both = jnp.dot(oht_ref[...], s2[...], preferred_element_type=f32)
-        r = both[:, :width] + both[:, width:]
-        d = cinv * r
-        result = d
-        rho_old = rho0
-        for turn in range(1, CHEB_COARSE):
-            r = r - gather(cycle * (CHEB_COARSE - 1) + turn - 1, d)
-            rho_new = 1.0 / (2.0 * THETA / DELTA - rho_old)
-            d = rho_new * rho_old * d + (2.0 * rho_new / DELTA) * (cinv * r)
-            result = result + d
-            rho_old = rho_new
-        hi, lo = split(result)
+        hi, lo = split(gather(cycle))
         packed = jnp.concatenate([hi, lo], axis=1)
 
         def spread(sl):
@@ -310,15 +387,21 @@
             xs[1, sl, :] = e
             sol_ref[sl, :] += e
 
-        apply(ex + 3, 0, prolong)
+        apply(ex, 0, prolong)
 
         def correct(sl, off):
             r = res_ref[sl, :] - (diag_ref[sl, :] * xs[1, sl, :] + off)
             res_ref[sl, :] = r
             xs[0, sl, :] = dinv_ref[sl, :] * r
 
-        apply(ex + 4, 1, correct)
-        smooth(ex + 5)
+        apply(ex + 1, 1, correct)
+        smooth(ex + 2)
+
+        @pl.when(cycle < CYCLES - 1)
+        def _():
+            smooth(ex + 4)
+            csend[cycle + 1] = restricted(ex + 6)
+
         return carry
 
     lax.fori_loop(0, CYCLES, cycle_body, 0)
@@ -331,34 +414,55 @@
     own = coarse_matrix[0]
     agg, coarse = own.shape
     a2, dinv, diag, oht, oh = run_setup(fine_values, columns, agg_map, block, agg)
-    exchanges = CYCLES * APPLIES
-    gathers = CYCLES * (CHEB_COARSE - 1)
+    start = lax.axis_index("sub") * agg
+    kept = (coarse // agg // 2 + 1) * agg
+    slab = lax.dynamic_slice_in_dim(jnp.concatenate([own, own], 1), start, kept, 1)
+    matrix = lax.all_gather(slab, "sub", axis=0, tiled=True)
     vmem = pl.BlockSpec(memory_space=pltpu.VMEM)
     smem = pl.BlockSpec(memory_space=pltpu.SMEM)
-    return pl.pallas_call(
-        functools.partial(main_kernel, n_grp, n_sub),
-        in_specs=[vmem] * 6 + [smem] * 2 + [vmem],
-        out_specs=[vmem] * 2,
-        out_shape=[jax.ShapeDtypeStruct((rows, width), f32)] * 2,
-        scratch_shapes=[
+    field = jax.ShapeDtypeStruct((rows, width), f32)
+
+    def scratch(exchanges):
+        return [
             pltpu.VMEM((2, rows, width), f32),
             pltpu.VMEM((rows + block, 2 * width), bf16),
             pltpu.VMEM((rows, 2 * width), bf16),
-            pltpu.VMEM((2 * agg, coarse), bf16),
             pltpu.VMEM((exchanges, 2, ghost, width), f32),
             pltpu.VMEM((exchanges, 2, ghost, width), f32),
-            pltpu.VMEM((gathers, agg, width), f32),
-            pltpu.VMEM((gathers, coarse, width), f32),
             pltpu.SemaphoreType.DMA((exchanges, 2)),
             pltpu.SemaphoreType.DMA((exchanges, 2)),
-            pltpu.SemaphoreType.DMA((gathers, n_sub)),
-            pltpu.SemaphoreType.DMA((gathers, n_sub)),
+        ]
+
+    def params(number):
+        return pltpu.CompilerParams(
+            collective_id=number, has_side_effects=True, vmem_limit_bytes=50 * 1024 * 1024
+        )
+
+    sol, res, crhs = pl.pallas_call(
+        functools.partial(main_kernel, True, n_grp, n_sub),
+        in_specs=[vmem] * 4 + [smem] * 2,
+        out_specs=[vmem] * 3,
+        out_shape=[field, field, jax.ShapeDtypeStruct((agg, width), f32)],
+        scratch_shapes=scratch(3),
+        compiler_params=params(0),
+        cost_estimate=pl.CostEstimate(flops=20_000_000_000, bytes_accessed=60_000_000, transcendentals=0),
+        name="opening",
+    )(right_side, a2, dinv, oht, send_lo, send_hi)
+    p2 = run_poly(matrix, agg)
+    return pl.pallas_call(
+        functools.partial(main_kernel, False, n_grp, n_sub),
+        in_specs=[vmem] * 8 + [smem] * 2 + [vmem],
+        out_specs=[vmem] * 2,
+        out_shape=[field] * 2,
+        scratch_shapes=scratch(CYCLES * APPLIES - 3) + [
+            pltpu.VMEM((CYCLES, agg, width), f32),
+            pltpu.VMEM((CYCLES, coarse, width), f32),
+            pltpu.SemaphoreType.DMA((CYCLES, n_sub)),
+            pltpu.SemaphoreType.DMA((CYCLES, n_sub)),
         ],
-        compiler_params=pltpu.CompilerParams(
-            collective_id=0, has_side_effects=True, vmem_limit_bytes=50 * 1024 * 1024
-        ),
+        compiler_params=params(1),
         name="cycles",
-    )(right_side, a2, dinv, diag, oht, oh, send_lo, send_hi, own)
+    )(sol, res, crhs, a2, dinv, diag, oht, oh, send_lo, send_hi, p2)
 
 
 def solution(mesh):

time: 219 us -> 163 us (0.74)
  Pallas kernels: 210 us -> 118 us
  waiting for transfers between devices: 0 us -> 19.8 us
  between operations: 0.65 us -> 14.1 us
    pallas_call x1 -> x3, Pallas kernels: 196 us -> 104 us  [the longest x1 78.8 us: body(): pl.pallas_call(functools.partial(main_kernel, False, n_grp, n_sub), in_sp...]
    all_gather x0 -> x1, waiting for transfers between devices: none -> 19.8 us  [body(): matrix = lax.all_gather(slab, 'sub', axis=0, tiled=True)]
    unnamed x12 -> x20, local copies, waits for them, and re-layouts: 6.37 us -> 6.73 us
  transfers between devices with their start and end apart: 0 -> 1, of which waited for: 0 -> 1; matrix products, arithmetic and copies ran while one was open for 0% -> 0% of each run, Pallas kernels for 0% -> 21%
where the time goes in v2:
time: 163 us; the launch traced here: 160 us
  Pallas kernels  118 us (72%)
  waiting for transfers between devices  19.8 us (12%)
  between operations  14.1 us (9%)
  local copies, waits for them, and re-layouts  6.73 us (4%)
  other arithmetic  1.78 us (1%)
    pallas_call x1, Pallas kernels, body(): pl.pallas_call(functools.partial(main_kernel, False, n_grp, n_sub), in_sp...  78.8 us
    pallas_call x1, Pallas kernels, body(): pl.pallas_call(functools.partial(main_kernel, True, n_grp, n_sub), in_spe...  19.9 us
    all_gather x1, waiting for transfers between devices, body(): matrix = lax.all_gather(slab, 'sub', axis=0, tiled=True)  19.8 us
    pallas_call x1, Pallas kernels, run_setup(): pl.pallas_call(setup_kernel, grid=(blocks,), in_specs=[pl.BlockSpec((entr...  14.3 us
    unnamed x20, local copies, waits for them, and re-layouts  6.73 us
    pallas_call x1, Pallas kernels, run_poly(): pl.pallas_call(poly_kernel, in_specs=[vmem], out_specs=vmem, out_shape=ja...  4.9 us
  transfers between devices with their start and end apart: 1, of which 1 were waited for; matrix products, arithmetic and copies ran while one was open for 0% of the time, Pallas kernels for 21%

profile of v2, /device:TPU:2, one launch (start us, length us, event | category | flops | bytes accessed | tf_op | source)
XLA Modules:
  0.0 160.4 jit_solution(16552040004302393081)
XLA Ops:
  7.2 0.0 all-gather.2.cloned.1.call-start
  7.2 1.8 %fusion = f32[128,640]{1,0:T(8,128)} fusion(s32[]{:T(128)S(6)} %select_n.3, f32[128,1024]{1,0:T(8,128)} %bitcast.2), kind=kLoop, calls=%fused_computation.2 | loop fusion | flops 81920 | bytes 851972 | tf_op jit(solution)/shard_map/concatenate | solution.py:419
  9.0 0.0 all-gather.2.cloned.1.call-update
  9.0 0.0 copy-start.6
  9.0 0.0 copy-start.7
  9.0 0.0 copy-start.8
  9.1 14.3 %setup.1 = (bf16[4096,256]{1,0:T(8,128)(2,1)}, f32[2048,128]{1,0:T(8,128)}, f32[2048,128]{1,0:T(8,128)}, bf16[128,2048]{1,0:T(8,128)(2,1)}, bf16[2048,128]{1,0:T(8,128)(2,1)}) custom-call(f32[81,2048]{1,0:T(8,128)} %fv_ref.1, s32[81,2048]{1,0:T(8,128)} %col_ref.1, s32[1,2048]{1,0:T(1,128)} %bitcast.3), custom_call_target="tpu_custom_call" | custom-call | flops 10000000000 | bytes 50000000 | tf_op jit(solution)/shard_map/setup/pallas_call | solution.py:84
  23.4 0.0 copy-done.6
  23.4 0.0 copy-done.7
  23.4 0.0 copy-done.8
  23.4 0.0 copy-start.3
  23.4 1.0 copy-done.3
  24.4 19.9 %opening.1 = (f32[2048,128]{1,0:T(8,128)S(1)}, f32[2048,128]{1,0:T(8,128)S(1)}, f32[128,128]{1,0:T(8,128)S(1)}) custom-call(f32[2048,128]{1,0:T(8,128)S(1)} %copy-done.8, bf16[4096,256]{1,0:T(8,128)(2,1)} %get-tuple-element.10.refs_1_.refs_3_, f32[2048,128]{1,0:T(8,128)} %get-tuple-element.11.refs_2_.refs_4_, bf16[128,2048]{1,0:T(8,128)(2,1)S(1)} %copy-done.3, ...), custom_call_target="tpu_custom_call" | custom-call | flops 20000000000 | bytes 60000000 | tf_op jit(solution)/shard_map/opening/pallas_call | solution.py:441
  44.4 0.0 copy-start.1
  44.4 1.0 copy-done.1
  45.4 0.0 copy-start.2
  45.4 1.0 copy-done.2
  46.4 19.8 %all-gather.2.cloned.1.call-done.m_ref = f32[1024,640]{1,0:T(8,128)} async-done(((f32[128,640]{1,0:T(8,128)}), f32[1024,640]{1,0:T(8,128)}) %all-gather.2.cloned.1.call-update) | async-done | bytes 2621456 | tf_op jit(solution)/shard_map/all_gather | solution.py:420
  66.2 0.0 copy-start
  66.2 1.7 %copy-done = f32[1024,640]{1,0:T(8,128)S(1)} copy-done((f32[1024,640]{1,0:T(8,128)S(1)}, f32[1024,640]{1,0:T(8,128)}, u32[]{:S(2)}) %copy-start) | copy-done | bytes 2621464
  67.9 0.0 copy-start.4
  67.9 0.0 copy-start.5
  67.9 4.9 %poly.1.refs_10_ = bf16[256,1024]{1,0:T(8,128)(2,1)S(1)} custom-call(f32[1024,640]{1,0:T(8,128)S(1)} %copy-done), custom_call_target="tpu_custom_call" | custom-call | tf_op jit(solution)/shard_map/poly/pallas_call | solution.py:160
  72.8 0.0 copy-done.4
  72.8 0.0 copy-done.5
  72.9 78.8 %cycles.1 = (f32[2048,128]{1,0:T(8,128)S(1)}, f32[2048,128]{1,0:T(8,128)S(1)}) custom-call(f32[2048,128]{1,0:T(8,128)} %copy-done.1, f32[2048,128]{1,0:T(8,128)} %copy-done.2, f32[128,128]{1,0:T(8,128)S(1)} %get-tuple-element.15.refs_2_, bf16[4096,256]{1,0:T(8,128)(2,1)} %get-tuple-element.10.refs_1_.refs_3_, f32[2048,128]{1,0:T(8,128)} %get-tuple-element.11.refs_2_.refs_4_, ...), custom_call_target="tpu_custom_call" | custom-call | tf_op jit(solution)/shard_map/cycles/pallas_call | solution.py:452
  151.6 1.0 copy.11
  152.6 1.0 copy.12
Async XLA Ops:
  7.2 59.0 %all-gather.2.cloned.1.call-start = ((), (), s32[]{:S(2)}) async-start(), calls=%async_computation | async-start | bytes 2949120 | tf_op jit(solution)/shard_map/all_gather | solution.py:420
  9.0 14.4 %copy-start.6 = (s32[64]{0:T(128)S(1)}, s32[64]{0:T(128)}, u32[]{:S(2)}) copy-start(s32[64]{0:T(128)} %refs_8_.1) | copy-start | bytes 772
  9.0 14.3 %copy-start.7 = (s32[64]{0:T(128)S(1)}, s32[64]{0:T(128)}, u32[]{:S(2)}) copy-start(s32[64]{0:T(128)} %refs_9_.1) | copy-start | bytes 772
  9.0 14.3 %copy-start.8 = (f32[2048,128]{1,0:T(8,128)S(1)}, f32[2048,128]{1,0:T(8,128)}, u32[]{:S(2)}) copy-start(f32[2048,128]{1,0:T(8,128)} %refs_0_.1) | copy-start | bytes 3145732
  23.4 1.0 copy-start.3
  44.4 1.0 copy-start.1
  45.4 1.0 copy-start.2
  66.2 1.7 %copy-start = (f32[1024,640]{1,0:T(8,128)S(1)}, f32[1024,640]{1,0:T(8,128)}, u32[]{:S(2)}) copy-start(f32[1024,640]{1,0:T(8,128)} %all-gather.2.cloned.1.call-done.m_ref) | copy-start | bytes 7864324
  67.9 4.9 %copy-start.4 = (bf16[128,2048]{1,0:T(8,128)(2,1)S(1)}, bf16[128,2048]{1,0:T(8,128)(2,1)}, u32[]{:S(2)}) copy-start(bf16[128,2048]{1,0:T(8,128)(2,1)} %get-tuple-element.12.refs_3_.refs_6_) | copy-start | bytes 1572868
  67.9 4.9 %copy-start.5 = (bf16[2048,128]{1,0:T(8,128)(2,1)S(1)}, bf16[2048,128]{1,0:T(8,128)(2,1)}, u32[]{:S(2)}) copy-start(bf16[2048,128]{1,0:T(8,128)(2,1)} %get-tuple-element.17.refs_7_) | copy-start | bytes 1572868
Sparse Core Ops, SparseCore 0:
  10.2 55.9 all-gather.1

commit v3 on v2

--- a/solution.py
+++ b/solution.py
@@ -314,18 +314,35 @@
         one(blocks - 1)
 
     def gather(step):
-        copies = []
-        for j in range(1, n_sub):
-            copies.append(pltpu.make_async_remote_copy(
-                src_ref=csend.at[step], dst_ref=whole.at[step, pl.ds(mine, agg)],
-                send_sem=csend_sem.at[step, j], recv_sem=crecv_sem.at[step, j],
-                device_id=(grp, lax.rem(me + j, n_sub)), device_id_type=MESH,
-            ))
+        half = n_sub // 2
+        partner = me + 1 - 2 * lax.rem(me, 2)
+
+        def block_copy(source, origin, slot, peer):
+            return pltpu.make_async_remote_copy(
+                src_ref=source, dst_ref=whole.at[step, pl.ds(pl.multiple_of(origin * agg, agg), agg)],
+                send_sem=csend_sem.at[step, slot], recv_sem=crecv_sem.at[step, slot],
+                device_id=(grp, peer), device_id_type=MESH,
+            )
+
+        copies = [block_copy(csend.at[step], me, 0, partner)]
+        for j in range(1, half):
+            copies.append(block_copy(csend.at[step], me, j, lax.rem(me + 2 * j, n_sub)))
         for copy in copies:
             copy.start()
         whole[step, pl.ds(mine, agg), :] = csend[step]
-        for copy in copies:
-            copy.wait()
+        passed = []
+        for j in range(1, half):
+            copies[j].wait_recv()
+            origin = lax.rem(me + n_sub - 2 * j, n_sub)
+            block_ref = whole.at[step, pl.ds(pl.multiple_of(origin * agg, agg), agg)]
+            copy = block_copy(block_ref, origin, half + j, partner)
+            copy.start()
+            passed.append(copy)
+        copies[0].wait_recv()
+        for copy in passed:
+            copy.wait_recv()
+        for copy in copies + passed:
+            copy.wait_send()
         hi, lo = split(whole[step])
         x = jnp.concatenate([hi, lo], axis=1)
         return quads(jnp.dot(m2[...], x, preferred_element_type=f32), agg, width)

time: 163 us -> 160 us (0.982)
  Pallas kernels: 118 us -> 116 us
    pallas_call x1, Pallas kernels: 78.8 us -> 76.7 us  [body(): pl.pallas_call(functools.partial(main_kernel, False, n_grp, n_sub), in_sp...]
  transfers between devices with their start and end apart: 1 -> 1, of which waited for: 1 -> 1; matrix products, arithmetic and copies ran while one was open for 0% -> 0% of each run, Pallas kernels for 21% -> 22%
where the time goes in v3:
time: 160 us; the launch traced here: 158 us
  Pallas kernels  116 us (72%)
  waiting for transfers between devices  19.8 us (12%)
  between operations  14.1 us (9%)
  local copies, waits for them, and re-layouts  6.73 us (4%)
  other arithmetic  1.78 us (1%)
    pallas_call x1, Pallas kernels, body(): pl.pallas_call(functools.partial(main_kernel, False, n_grp, n_sub), in_sp...  76.7 us
    pallas_call x1, Pallas kernels, body(): pl.pallas_call(functools.partial(main_kernel, True, n_grp, n_sub), in_spe...  19.9 us
    all_gather x1, waiting for transfers between devices, body(): matrix = lax.all_gather(slab, 'sub', axis=0, tiled=True)  19.8 us
    pallas_call x1, Pallas kernels, run_setup(): pl.pallas_call(setup_kernel, grid=(blocks,), in_specs=[pl.BlockSpec((entr...  14.3 us
    unnamed x20, local copies, waits for them, and re-layouts  6.73 us
    pallas_call x1, Pallas kernels, run_poly(): pl.pallas_call(poly_kernel, in_specs=[vmem], out_specs=vmem, out_shape=ja...  4.9 us
  transfers between devices with their start and end apart: 1, of which 1 were waited for; matrix products, arithmetic and copies ran while one was open for 0% of the time, Pallas kernels for 22%

profile of v3, /device:TPU:2, one launch (start us, length us, event | category | flops | bytes accessed | tf_op | source)
XLA Modules:
  0.0 158.4 jit_solution(818107915916461572)
XLA Ops:
  7.2 0.0 all-gather.2.cloned.1.call-start
  7.2 1.8 %fusion = f32[128,640]{1,0:T(8,128)} fusion(s32[]{:T(128)S(6)} %select_n.3, f32[128,1024]{1,0:T(8,128)} %bitcast.2), kind=kLoop, calls=%fused_computation.2 | loop fusion | flops 81920 | bytes 851972 | tf_op jit(solution)/shard_map/concatenate | solution.py:436
  9.0 0.0 all-gather.2.cloned.1.call-update
  9.0 0.0 copy-start.6
  9.0 0.0 copy-start.7
  9.0 0.0 copy-start.8
  9.1 14.3 %setup.1 = (bf16[4096,256]{1,0:T(8,128)(2,1)}, f32[2048,128]{1,0:T(8,128)}, f32[2048,128]{1,0:T(8,128)}, bf16[128,2048]{1,0:T(8,128)(2,1)}, bf16[2048,128]{1,0:T(8,128)(2,1)}) custom-call(f32[81,2048]{1,0:T(8,128)} %fv_ref.1, s32[81,2048]{1,0:T(8,128)} %col_ref.1, s32[1,2048]{1,0:T(1,128)} %bitcast.3), custom_call_target="tpu_custom_call" | custom-call | flops 10000000000 | bytes 50000000 | tf_op jit(solution)/shard_map/setup/pallas_call | solution.py:84
  23.4 0.0 copy-done.6
  23.4 0.0 copy-done.7
  23.4 0.0 copy-done.8
  23.4 0.0 copy-start.3
  23.4 1.0 copy-done.3
  24.4 19.9 %opening.1 = (f32[2048,128]{1,0:T(8,128)S(1)}, f32[2048,128]{1,0:T(8,128)S(1)}, f32[128,128]{1,0:T(8,128)S(1)}) custom-call(f32[2048,128]{1,0:T(8,128)S(1)} %copy-done.8, bf16[4096,256]{1,0:T(8,128)(2,1)} %get-tuple-element.10.refs_1_.refs_3_, f32[2048,128]{1,0:T(8,128)} %get-tuple-element.11.refs_2_.refs_4_, bf16[128,2048]{1,0:T(8,128)(2,1)S(1)} %copy-done.3, ...), custom_call_target="tpu_custom_call" | custom-call | flops 20000000000 | bytes 60000000 | tf_op jit(solution)/shard_map/opening/pallas_call | solution.py:458
  44.4 0.0 copy-start.1
  44.4 1.0 copy-done.1
  45.4 0.0 copy-start.2
  45.4 1.0 copy-done.2
  46.4 19.8 %all-gather.2.cloned.1.call-done.m_ref = f32[1024,640]{1,0:T(8,128)} async-done(((f32[128,640]{1,0:T(8,128)}), f32[1024,640]{1,0:T(8,128)}) %all-gather.2.cloned.1.call-update) | async-done | bytes 2621456 | tf_op jit(solution)/shard_map/all_gather | solution.py:437
  66.2 0.0 copy-start
  66.2 1.7 %copy-done = f32[1024,640]{1,0:T(8,128)S(1)} copy-done((f32[1024,640]{1,0:T(8,128)S(1)}, f32[1024,640]{1,0:T(8,128)}, u32[]{:S(2)}) %copy-start) | copy-done | bytes 2621464
  67.9 0.0 copy-start.4
  67.9 0.0 copy-start.5
  67.9 4.9 %poly.1.refs_10_ = bf16[256,1024]{1,0:T(8,128)(2,1)S(1)} custom-call(f32[1024,640]{1,0:T(8,128)S(1)} %copy-done), custom_call_target="tpu_custom_call" | custom-call | tf_op jit(solution)/shard_map/poly/pallas_call | solution.py:160
  72.8 0.0 copy-done.4
  72.8 0.0 copy-done.5
  72.9 76.7 %cycles.1 = (f32[2048,128]{1,0:T(8,128)S(1)}, f32[2048,128]{1,0:T(8,128)S(1)}) custom-call(f32[2048,128]{1,0:T(8,128)} %copy-done.1, f32[2048,128]{1,0:T(8,128)} %copy-done.2, f32[128,128]{1,0:T(8,128)S(1)} %get-tuple-element.15.refs_2_, bf16[4096,256]{1,0:T(8,128)(2,1)} %get-tuple-element.10.refs_1_.refs_3_, f32[2048,128]{1,0:T(8,128)} %get-tuple-element.11.refs_2_.refs_4_, ...), custom_call_target="tpu_custom_call" | custom-call | tf_op jit(solution)/shard_map/cycles/pallas_call | solution.py:469
  149.6 1.0 copy.11
  150.6 1.0 copy.12
Async XLA Ops:
  7.2 59.0 %all-gather.2.cloned.1.call-start = ((), (), s32[]{:S(2)}) async-start(), calls=%async_computation | async-start | bytes 2949120 | tf_op jit(solution)/shard_map/all_gather | solution.py:437
  9.0 14.4 %copy-start.6 = (s32[64]{0:T(128)S(1)}, s32[64]{0:T(128)}, u32[]{:S(2)}) copy-start(s32[64]{0:T(128)} %refs_8_.1) | copy-start | bytes 772
  9.0 14.3 %copy-start.7 = (s32[64]{0:T(128)S(1)}, s32[64]{0:T(128)}, u32[]{:S(2)}) copy-start(s32[64]{0:T(128)} %refs_9_.1) | copy-start | bytes 772
  9.0 14.3 %copy-start.8 = (f32[2048,128]{1,0:T(8,128)S(1)}, f32[2048,128]{1,0:T(8,128)}, u32[]{:S(2)}) copy-start(f32[2048,128]{1,0:T(8,128)} %refs_0_.1) | copy-start | bytes 3145732
  23.4 1.0 copy-start.3
  44.4 1.0 copy-start.1
  45.4 1.0 copy-start.2
  66.2 1.7 %copy-start = (f32[1024,640]{1,0:T(8,128)S(1)}, f32[1024,640]{1,0:T(8,128)}, u32[]{:S(2)}) copy-start(f32[1024,640]{1,0:T(8,128)} %all-gather.2.cloned.1.call-done.m_ref) | copy-start | bytes 7864324
  67.9 4.9 %copy-start.4 = (bf16[128,2048]{1,0:T(8,128)(2,1)S(1)}, bf16[128,2048]{1,0:T(8,128)(2,1)}, u32[]{:S(2)}) copy-start(bf16[128,2048]{1,0:T(8,128)(2,1)} %get-tuple-element.12.refs_3_.refs_6_) | copy-start | bytes 1572868
  67.9 4.9 %copy-start.5 = (bf16[2048,128]{1,0:T(8,128)(2,1)S(1)}, bf16[2048,128]{1,0:T(8,128)(2,1)}, u32[]{:S(2)}) copy-start(bf16[2048,128]{1,0:T(8,128)(2,1)} %get-tuple-element.17.refs_7_) | copy-start | bytes 1572868
Sparse Core Ops, SparseCore 0:
  10.2 55.9 all-gather.1
